TPU v7x, 32 devices: a whole 2x2x4 slice. The times are simulated.
32 devices in a mesh: tiles: 2 (over x), morton: 16 (over z, y, core).
Axes of the slice: x: 2, y: 2, z: 4, core: 2. Of those that a mesh axis runs over, the one named last changes fastest.
Arguments:
- features: bfloat16 [256, 512, 64], P(('tiles', 'morton')), parts along dimension 0, may hold values from -6 to 6
- neighbours: int32 [256, 27], P(('tiles', 'morton')), parts along dimension 0, may hold values from -1 to 127, as said below
- occupancy: int32 [256, 16], P(('tiles', 'morton')), parts along dimension 0, may hold values from -2147483648 to 2147483647, as said below
- conv_one: bfloat16 [27, 64, 64], replicated, may hold values from -0.21875 to 0.21875
- first_reduce_kernel: bfloat16 [8, 64, 128], replicated, may hold values from -0.5 to 0.5
- conv_two: bfloat16 [27, 128, 128], replicated, may hold values from -0.1875 to 0.1875
- second_reduce_kernel: bfloat16 [8, 128, 256], replicated, may hold values from -0.375 to 0.375
- conv_three: bfloat16 [27, 256, 256], replicated, may hold values from -0.125 to 0.125
Outputs:
- first_level_features: bfloat16 [256, 512, 64], P(('tiles', 'morton')), parts along dimension 0
- second_level_features: bfloat16 [256, 64, 128], P(('tiles', 'morton')), parts along dimension 0
- skip_three: bfloat16 [256, 8, 256], P(('tiles', 'morton')), parts along dimension 0
There are 2 independent parts, one for each index of `tiles`. A program takes and returns all parts, laid end to end along the dimension named above; an argument that names none is the same for every part. Nothing has to cross between parts.
Inputs may be any that keep to these rules, and one draw needn't show every extreme that they name: `neighbours`: bricks are numbered by x slice, then by cell of the slice's 4 x 4 cross-section in rising order, 8 occupied bricks to a slice. Entry 9 (a+1) + 3 (c+1) + (e+1) of a brick's row is the number of the brick at offset (a, c, e), or -1 if that cell is empty or outside the tile; entry 13 is the brick itself. Every neighbour lies in the brick's own slice or in an adjacent one. Bit k, the lowest being bit 0, of word w of a brick's row is the occupancy of voxel 32 w + k; bit 31 is the sign bit of the word.
All inputs are finite; a program needn't handle non-finite values.
Results may differ from a plain program's by a relative error of at most 0.008.
Values may be sent and summed in bfloat16 or wider, within the bound.
No kernel may reach another device: no remote copies, remote signals or barrier semaphores. Data moves between devices by JAX's collectives and lax.ppermute only.
A program may use at most 128 MiB of HBM per device.

v0:
```python
import jax
import jax.numpy as jnp
import numpy as np
from jax import lax
from jax.experimental import pallas as pl
from jax.experimental.pallas import tpu as pltpu
from jax.sharding import PartitionSpec as P

F32 = jnp.float32
BF16 = jnp.bfloat16
TAPS = [(a, c, e) for a in range(3) for c in range(3) for e in range(3)]


def dot(x, y):
    return jnp.dot(x, y, preferred_element_type=F32)


def iota(shape, axis):
    return lax.broadcasted_iota(jnp.int32, shape, axis)


def slot_of(neighbours, first, count, b, tap):
    number = neighbours[b, tap]
    shift = (1 - tap // 9) * count
    return jnp.where(number < 0, count, number - first[0] + shift)


def bits_of(words, shift):
    return jnp.bitwise_and(lax.shift_right_logical(words, shift), 1).astype(F32)


def column_mask(occupancy, b, column):
    lane = iota((1, 128), 1)
    w = [jnp.full((1, 128), occupancy[b, 4 * column + q], jnp.int32) for q in range(4)]
    words = jnp.where(
        lane < 64, jnp.where(lane < 32, w[0], w[1]), jnp.where(lane < 96, w[2], w[3])
    )
    return bits_of(words, jnp.bitwise_and(lane, 31))


def spread_pairs(word):
    word = jnp.bitwise_or(word, lax.shift_right_logical(word, 1))
    return jnp.bitwise_or(word, lax.shift_right_logical(word, 8))


def mask_two_word(occupancy, b, i, half):
    return spread_pairs(
        jnp.bitwise_or(occupancy[b, 4 * i + half], occupancy[b, 4 * i + 2 + half])
    )


def mask_two_tile(occupancy, b, i):
    row = iota((8, 128), 0)
    shift = 16 * (row // 4) + 2 * (row % 4)
    return jnp.concatenate(
        [
            bits_of(jnp.full((8, 128), mask_two_word(occupancy, b, i, half), jnp.int32), shift)
            for half in range(2)
        ],
        axis=0,
    )


def mask_three_tile(occupancy, b):
    row = iota((8, 128), 0)
    tile = jnp.zeros((8, 128), jnp.int32)
    for i in range(2):
        for j in range(2):
            word = jnp.bitwise_or(
                mask_two_word(occupancy, b, 2 * i, j), mask_two_word(occupancy, b, 2 * i + 1, j)
            )
            word = jnp.bitwise_or(word, lax.shift_right_logical(word, 16))
            word = jnp.bitwise_or(word, lax.shift_right_logical(word, 2))
            tile = jnp.where(row // 2 == 2 * i + j, word, tile)
    return bits_of(tile, 4 * (row % 2))


def faces_kernel(odd, occupancy, first_columns, last_columns, to_a, to_b):
    count = first_columns.shape[0]
    lane = iota((64, 128), 1)
    is_odd = odd[0] == 1
    for q in range(count // 2):
        low, high = [], []
        for b in (2 * q, 2 * q + 1):
            low.append(first_columns[b].astype(F32) * column_mask(occupancy, b, 0))
            high.append(last_columns[b].astype(F32) * column_mask(occupancy, b, 3))
        lows = jnp.where(lane < 64, low[0], pltpu.roll(low[1], 64, 1))
        highs = jnp.where(lane < 64, pltpu.roll(high[0], 64, 1), high[1])
        to_a[q] = jnp.where(is_odd, lows, highs).astype(BF16)
        to_b[q] = jnp.where(is_odd, highs, lows).astype(BF16)


def level_one_kernel(
    odd, first, neighbours, occupancy, features, from_a, from_b, kernel, reduce,
    out, second, to_a, to_b,
    pairs, wrap, halo, padded, taps, low_sums, high_sums,
):
    count = features.shape[0]
    lane = iota((64, 128), 1)
    small = iota((8, 128), 1)
    row = iota((8, 128), 0)
    is_odd = odd[0] == 1

    for c in range(3):
        for e in range(3):
            w = [kernel[9 * a + 3 * c + e].astype(F32) for a in range(3)]
            none = jnp.zeros((64, 64), F32)
            for p in range(4):
                left = w[p] if p < 3 else none
                right = w[p - 1] if p > 0 else none
                block = jnp.concatenate([left, right], axis=1).astype(BF16)
                taps[(3 * c + e) * 256 + p * 64 : (3 * c + e) * 256 + (p + 1) * 64, :] = block

    for table in (pairs.at[0], pairs.at[1], pairs.at[2], wrap, halo):
        table[count] = jnp.zeros((64, 128), F32)
    for b in range(count):
        cols = [
            features[b, :, 128 * q : 128 * (q + 1)].astype(F32) * column_mask(occupancy, b, q)
            for q in range(4)
        ]
        rolled = [pltpu.roll(col, 64, 1) for col in cols]
        m = jnp.concatenate(
            [
                jnp.where(lane < 64, rolled[0], cols[1]),
                jnp.where(lane < 64, cols[1], rolled[2]),
            ],
            axis=0,
        ).T
        pairs[0, b] = m[:64]
        pairs[1, b] = m[64:]
        m = jnp.concatenate(
            [
                jnp.where(lane < 64, rolled[2], cols[3]),
                jnp.where(lane < 64, cols[3], rolled[0]),
            ],
            axis=0,
        ).T
        pairs[2, b] = m[:64]
        wrap[b] = m[64:]
    for q in range(count // 2):
        one, two = from_a[q].astype(F32), from_b[q].astype(F32)
        m = jnp.concatenate(
            [jnp.where(is_odd, one, two), jnp.where(is_odd, two, one)], axis=0
        ).T
        halo[2 * q] = m[:64]
        halo[2 * q + 1] = m[64:]

    weights = jnp.concatenate(
        [
            jnp.concatenate(
                [
                    jnp.concatenate([reduce[4 * ci + 2 * cj], reduce[4 * ci + 2 * cj + 1]], axis=1)
                    for ci in range(2)
                ],
                axis=0,
            )
            for cj in range(2)
        ],
        axis=0,
    )

    def brick(b, carry):
        slot = [slot_of(neighbours, first, count, b, tap) for tap in range(27)]

        def source(pair, j, e):
            c, j = (0, 7) if j < 0 else (2, 0) if j > 7 else (1, j)
            rows = pl.ds(8 * j, 8)
            own = slot[9 + 3 * c + e]
            if pair == 0:
                return jnp.where(
                    small < 64, halo[slot[3 * c + e], rows, :], wrap[own, rows, :]
                )
            if pair == 4:
                return jnp.where(
                    small < 64, wrap[own, rows, :], halo[slot[18 + 3 * c + e], rows, :]
                )
            return pairs[pair - 1, own, rows, :]

        for pair in range(5):
            shifted = []
            for j in range(-1, 9):
                left, mid, right = [source(pair, j, e) for e in range(3)]
                shifted.append(
                    (
                        pltpu.roll(jnp.where(row == 7, left, mid), 1, 0),
                        mid,
                        pltpu.roll(jnp.where(row == 0, right, mid), 7, 0),
                    )
                )
            for jr in range(6):
                for e in range(3):
                    padded[e, pair, jr] = jnp.concatenate(
                        [shifted[jr][e], shifted[jr + 4][e]], axis=0
                    ).astype(BF16)

        columns = []
        for c in range(3):
            for e in range(3):
                for p in range(2):
                    columns.append(padded[e, p : p + 4, c : c + 4].reshape(256, 128))
        total = dot(jnp.concatenate(columns, axis=1), taps[...])

        tiles = {}
        for i in range(4):
            for jr in range(4):
                for half in range(2):
                    at = (i * 4 + jr) * 16 + half * 8
                    words = jnp.where(
                        small < 64, occupancy[b, 4 * i + half], occupancy[b, 4 * i + 2 + half]
                    )
                    tiles[i, 4 * half + jr] = jnp.maximum(total[at : at + 8], 0.0) * bits_of(
                        words, row + 8 * jr
                    )
        for i in (0, 2):
            m = jnp.concatenate(
                [tiles[i + q, j] for q in range(2) for j in range(8)], axis=0
            ).T
            top, bottom = m[:64], m[64:]
            out[b, :, 128 * i : 128 * (i + 1)] = jnp.where(
                lane < 64, top, pltpu.roll(bottom, 64, 1)
            ).astype(BF16)
            out[b, :, 128 * (i + 1) : 128 * (i + 2)] = jnp.where(
                lane < 64, pltpu.roll(top, 64, 1), bottom
            ).astype(BF16)

        left = jnp.concatenate(
            [
                jnp.concatenate(
                    [
                        jnp.concatenate([tiles[i, j], tiles[i, j + 1]], axis=1)
                        for j in (0, 2, 4, 6)
                    ],
                    axis=0,
                )
                for i in range(4)
            ],
            axis=0,
        ).astype(BF16)
        sums = dot(left, weights)
        low_sums[...] = sums[:, :128]
        high_sums[...] = sums[:, 128:]
        planes = []
        for i in range(4):
            plane = (
                low_sums[pl.ds(32 * i, 16, stride=2), :]
                + high_sums[pl.ds(32 * i + 1, 16, stride=2), :]
            )
            plane = (jnp.maximum(plane, 0.0) * mask_two_tile(occupancy, b, i)).astype(BF16)
            second[b, i] = plane
            planes.append(plane)
        to_a[b] = jnp.where(is_odd, planes[0], planes[3])
        to_b[b] = jnp.where(is_odd, planes[3], planes[0])
        return carry

    lax.fori_loop(0, count, brick, 0)


def level_two_kernel(
    odd, first, neighbours, occupancy, shifts, children, inputs, from_a, from_b, kernel, reduce,
    out, third,
    table, low, high, windows,
):
    count = inputs.shape[0]
    is_odd = odd[0] == 1
    for i in range(4):
        table[count, i] = jnp.zeros((16, 128), BF16)
    low[count] = jnp.zeros((16, 128), BF16)
    high[count] = jnp.zeros((16, 128), BF16)
    for b in range(count):
        table[b] = inputs[b]
        low[b] = jnp.where(is_odd, from_a[b], from_b[b])
        high[b] = jnp.where(is_odd, from_b[b], from_a[b])

    for b in range(count):
        slot = [slot_of(neighbours, first, count, b, tap) for tap in range(27)]
        planes = [jnp.concatenate([low[slot[q]] for q in range(9)], axis=0)]
        for i in range(4):
            planes.append(jnp.concatenate([table[slot[9 + q], i] for q in range(9)], axis=0))
        planes.append(jnp.concatenate([high[slot[18 + q]] for q in range(9)], axis=0))
        moved = dot(shifts[...], jnp.concatenate(planes, axis=1)).astype(BF16)
        for q in range(9):
            for i in range(6):
                windows[q, b, i] = moved[16 * q : 16 * (q + 1), 128 * i : 128 * (i + 1)]

    total = dot(
        jnp.concatenate(
            [
                windows[3 * c + e, :, a : a + 4].reshape(count * 64, 128)
                for a, c, e in TAPS
            ],
            axis=1,
        ),
        kernel[...].reshape(27 * 128, 128),
    )
    bricks = []
    for b in range(count):
        mask = jnp.concatenate([mask_two_tile(occupancy, b, i) for i in range(4)], axis=0)
        brick = (jnp.maximum(total[64 * b : 64 * (b + 1)], 0.0) * mask).astype(BF16)
        out[b] = brick
        bricks.append(brick)
    moved = dot(children[...], jnp.concatenate(bricks, axis=1))
    left = jnp.concatenate(
        [
            jnp.concatenate(
                [moved[8 * q : 8 * (q + 1), 128 * b : 128 * (b + 1)] for b in range(count)], axis=0
            )
            for q in range(8)
        ],
        axis=1,
    ).astype(BF16)
    sums = jnp.maximum(dot(left, reduce[...].reshape(8 * 128, 256)), 0.0)
    for b in range(count):
        mask = mask_three_tile(occupancy, b)
        mask = jnp.concatenate([mask, mask], axis=1)
        third[b] = (sums[8 * b : 8 * (b + 1)] * mask).astype(BF16)


def level_three_kernel(
    odd, first, neighbours, occupancy, shifts, inputs, from_a, from_b, kernel,
    out,
    table,
):
    count = inputs.shape[0]
    is_odd = odd[0] == 1
    for a in range(3):
        table[a, count] = jnp.zeros((8, 256), F32)
    for b in range(count):
        one, two = from_a[b].astype(F32), from_b[b].astype(F32)
        table[0, b] = jnp.where(is_odd, one, two)
        table[1, b] = inputs[b].astype(F32)
        table[2, b] = jnp.where(is_odd, two, one)
    bricks = []
    for b in range(count):
        bricks.append(
            jnp.concatenate(
                [
                    table[tap // 9, slot_of(neighbours, first, count, b, tap)]
                    for tap in range(27)
                ],
                axis=0,
            ).astype(BF16)
        )
    moved = dot(shifts[...], jnp.concatenate(bricks, axis=1))
    left = jnp.concatenate(
        [
            jnp.concatenate(
                [moved[8 * q : 8 * (q + 1), 256 * b : 256 * (b + 1)] for b in range(count)], axis=0
            )
            for q in range(27)
        ],
        axis=1,
    ).astype(BF16)
    sums = jnp.maximum(dot(left, kernel[...].reshape(27 * 256, 256)), 0.0)
    for b in range(count):
        mask = mask_three_tile(occupancy, b)
        mask = jnp.concatenate([mask, mask], axis=1)
        out[b] = (sums[8 * b : 8 * (b + 1)] * mask).astype(BF16)


def plane_shifts():
    pick = np.zeros((144, 144), np.float32)
    for c in range(3):
        for e in range(3):
            for j in range(4):
                for k in range(4):
                    y, z = j + c - 1, k + e - 1
                    brick = 3 * (y // 4 + 1) + z // 4 + 1
                    pick[(3 * c + e) * 16 + 4 * j + k, brick * 16 + 4 * (y % 4) + z % 4] = 1
    return jnp.asarray(pick, BF16)


def child_rows():
    pick = np.zeros((64, 64), np.float32)
    for q in range(8):
        for u in range(8):
            x, y, z = [2 * ((u >> s) & 1) + ((q >> s) & 1) for s in (2, 1, 0)]
            pick[8 * q + u, 16 * x + 4 * y + z] = 1
    return jnp.asarray(pick, BF16)


def brick_shifts():
    pick = np.zeros((216, 216), np.float32)
    for tap, (a, c, e) in enumerate(TAPS):
        for u in range(8):
            x, y, z = (u >> 2) + a - 1, ((u >> 1) & 1) + c - 1, (u & 1) + e - 1
            brick = 9 * (x // 2 + 1) + 3 * (y // 2 + 1) + z // 2 + 1
            pick[8 * tap + u, 8 * brick + 4 * (x % 2) + 2 * (y % 2) + z % 2] = 1
    return jnp.asarray(pick, BF16)


SMEM = pl.BlockSpec(memory_space=pltpu.SMEM)
VMEM = pl.BlockSpec(memory_space=pltpu.VMEM)
PARAMS = pltpu.CompilerParams(vmem_limit_bytes=48 * 1024 * 1024)


def swaps(tiles, count):
    inner, outer = [], []
    for t in range(tiles):
        for m in range(count):
            if m ^ 1 < count:
                inner.append((t * count + m, t * count + (m ^ 1)))
            other = ((m - 1) ^ 1) + 1 if m else -1
            if 0 <= other < count:
                outer.append((t * count + m, t * count + other))
            elif t ^ 1 < tiles:
                outer.append((t * count + m, (t ^ 1) * count + m))
    return inner, outer


def on_device(
    features,
    neighbours,
    occupancy,
    conv_one,
    first_reduce_kernel,
    conv_two,
    second_reduce_kernel,
    conv_three,
):
    axes = ("tiles", "morton")
    inner, outer = swaps(lax.axis_size("tiles"), lax.axis_size("morton"))
    count = features.shape[0]
    place = lax.axis_index("morton")
    odd = jnp.reshape(place % 2, (1,)).astype(jnp.int32)
    first = jnp.reshape(place * count, (1,)).astype(jnp.int32)
    features = jnp.swapaxes(features, 1, 2)

    def exchange(to_a, to_b):
        from_b = lax.ppermute(to_b, axes, outer)
        return lax.ppermute(to_a, axes, inner), from_b

    face = jax.ShapeDtypeStruct((count // 2, 64, 128), BF16)
    edge = pl.BlockSpec((count, 64, 128), lambda i: (0, 0, 0))
    to_a, to_b = pl.pallas_call(
        faces_kernel,
        grid=(1,),
        out_shape=(face, face),
        in_specs=[SMEM, SMEM, edge, pl.BlockSpec((count, 64, 128), lambda i: (0, 0, 3))],
        out_specs=(pl.BlockSpec((count // 2, 64, 128), lambda i: (0, 0, 0)),) * 2,
        compiler_params=PARAMS,
    )(odd, occupancy, features, features)
    from_a, from_b = exchange(to_a, to_b)

    plane = jax.ShapeDtypeStruct((count, 16, 128), BF16)
    first_level, second_input, to_a, to_b = pl.pallas_call(
        level_one_kernel,
        out_shape=(
            jax.ShapeDtypeStruct((count, 64, 512), BF16),
            jax.ShapeDtypeStruct((count, 4, 16, 128), BF16),
            plane,
            plane,
        ),
        in_specs=[SMEM] * 4 + [VMEM] * 5,
        out_specs=(VMEM,) * 4,
        scratch_shapes=[
            pltpu.VMEM((3, count + 1, 64, 128), F32),
            pltpu.VMEM((count + 1, 64, 128), F32),
            pltpu.VMEM((count + 1, 64, 128), F32),
            pltpu.VMEM((3, 5, 6, 16, 128), BF16),
            pltpu.VMEM((9 * 256, 128), BF16),
            pltpu.VMEM((128, 128), F32),
            pltpu.VMEM((128, 128), F32),
        ],
        compiler_params=PARAMS,
    )(
        odd, first, neighbours, occupancy, features, from_a, from_b, conv_one,
        first_reduce_kernel,
    )
    from_a, from_b = exchange(to_a, to_b)

    second_level, third_input = pl.pallas_call(
        level_two_kernel,
        out_shape=(
            jax.ShapeDtypeStruct((count, 64, 128), BF16),
            jax.ShapeDtypeStruct((count, 8, 256), BF16),
        ),
        in_specs=[SMEM] * 4 + [VMEM] * 7,
        out_specs=(VMEM,) * 2,
        scratch_shapes=[
            pltpu.VMEM((count + 1, 4, 16, 128), BF16),
            pltpu.VMEM((count + 1, 16, 128), BF16),
            pltpu.VMEM((count + 1, 16, 128), BF16),
            pltpu.VMEM((9, count, 6, 16, 128), BF16),
        ],
        compiler_params=PARAMS,
    )(
        odd, first, neighbours, occupancy, plane_shifts(), child_rows(), second_input,
        from_a, from_b, conv_two, second_reduce_kernel,
    )
    from_a, from_b = exchange(third_input, third_input)

    third_level = pl.pallas_call(
        level_three_kernel,
        out_shape=jax.ShapeDtypeStruct((count, 8, 256), BF16),
        in_specs=[SMEM] * 4 + [VMEM] * 5,
        out_specs=VMEM,
        scratch_shapes=[pltpu.VMEM((3, count + 1, 8, 256), F32)],
        compiler_params=PARAMS,
    )(
        odd, first, neighbours, occupancy, brick_shifts(), third_input, from_a, from_b,
        conv_three,
    )
    return jnp.swapaxes(first_level, 1, 2), second_level, third_level


def solution(mesh):
    split = P(("tiles", "morton"))
    return jax.shard_map(
        on_device,
        mesh=mesh,
        in_specs=(split, split, split, P(), P(), P(), P(), P()),
        out_specs=(split, split, split),
        check_vma=False,
    )
```

profile of v0, /device:TPU:21, one launch (start us, length us, event | category | flops | bytes accessed | tf_op | source)
XLA Modules:
  0.0 41.3 jit_solution(9317553929502680233)
XLA Ops:
  0.6 0.0 copy-start
  0.7 1.0 %copy-done = bf16[8,512,64]{1,2,0:T(8,128)(2,1)S(1)} copy-done((bf16[8,512,64]{1,2,0:T(8,128)(2,1)S(1)}, bf16[8,512,64]{1,2,0:T(8,128)(2,1)}, u32[]{:S(2)}) %copy-start) | copy-done | bytes 524312
  1.7 0.0 copy-start.9
  1.7 0.7 %copy-done.9 = s32[8,16]{1,0:T(8,128)S(1)} copy-done((s32[8,16]{1,0:T(8,128)S(1)}, s32[8,16]{1,0:T(8,128)}, u32[]{:S(2)}) %copy-start.9) | copy-done | bytes 536
  2.4 0.0 copy-start.7
  2.4 0.7 %shard_map.130 = (bf16[4,64,128]{2,1,0:T(8,128)(2,1)S(1)}, bf16[4,64,128]{2,1,0:T(8,128)(2,1)S(1)}) custom-call(s32[1]{0:T(128)} %bitcast.odd, s32[8,16]{1,0:T(8,128)S(1)} %copy-done.9, bf16[8,64,512]{2,1,0:T(8,128)(2,1)S(1)} %bitcast.4, bf16[8,64,512]{2,1,0:T(8,128)(2,1)S(1)} %bitcast.5), custom_call_target="tpu_custom_call" | custom-call | tf_op jit(solution)/shard_map/pallas_call | solution.py:434
  3.1 0.7 %collective-permute-start = (bf16[4,64,128]{2,1,0:T(8,128)(2,1)S(1)}, bf16[4,64,128]{2,1,0:T(8,128)(2,1)S(1)}, u32[]{:S(2)}, u32[]{:S(2)}) collective-permute-start(bf16[4,64,128]{2,1,0:T(8,128)(2,1)S(1)} %get-tuple-element.11), channel_id=1, source_target_pairs={{0,1},{1,0},{2,3},{3,2},{4,5},{5,4},{6,7},{7,6},{8,9},{9,8},{10,11... | collective-permute-start | bytes 196616 | tf_op jit(solution)/shard_map/ppermute | solution.py:430
  3.8 1.2 %collective-permute-start.1 = (bf16[4,64,128]{2,1,0:T(8,128)(2,1)S(1)}, bf16[4,64,128]{2,1,0:T(8,128)(2,1)S(1)}, u32[]{:S(2)}, u32[]{:S(2)}) collective-permute-start(bf16[4,64,128]{2,1,0:T(8,128)(2,1)S(1)} %get-tuple-element.12), channel_id=1, source_target_pairs={{0,16},{1,2},{2,1},{3,4},{4,3},{5,6},{6,5},{7,8},{8,7},{9,10},{10,... | collective-permute-start | bytes 196616 | tf_op jit(solution)/shard_map/ppermute | solution.py:429
  5.0 0.0 collective-permute-done.from_a
  5.0 3.4 %collective-permute-done.1.from_b = bf16[4,64,128]{2,1,0:T(8,128)(2,1)S(1)} collective-permute-done((bf16[4,64,128]{2,1,0:T(8,128)(2,1)S(1)}, bf16[4,64,128]{2,1,0:T(8,128)(2,1)S(1)}, u32[]{:S(2)}, u32[]{:S(2)}) %collective-permute-start.1) | collective-permute-done | bytes 65568 | tf_op jit(solution)/shard_map/ppermute | solution.py:429
  8.4 0.0 copy-start.1
  8.4 1.0 %copy-done.1 = bf16[8,512,64]{1,2,0:T(8,128)(2,1)S(1)} copy-done((bf16[8,512,64]{1,2,0:T(8,128)(2,1)S(1)}, bf16[8,512,64]{1,2,0:T(8,128)(2,1)}, u32[]{:S(2)}) %copy-start.1) | copy-done | bytes 524312
  9.5 0.0 copy-start.5
  9.5 1.0 %copy-done.5 = bf16[27,64,64]{2,1,0:T(8,128)(2,1)S(1)} copy-done((bf16[27,64,64]{2,1,0:T(8,128)(2,1)S(1)}, bf16[27,64,64]{2,1,0:T(8,128)(2,1)}, u32[]{:S(2)}) %copy-start.5) | copy-done | bytes 221208
  10.5 0.0 copy-start.6
  10.5 0.9 %copy-done.6 = bf16[8,64,128]{2,1,0:T(8,128)(2,1)S(1)} copy-done((bf16[8,64,128]{2,1,0:T(8,128)(2,1)S(1)}, bf16[8,64,128]{2,1,0:T(8,128)(2,1)}, u32[]{:S(2)}) %copy-start.6) | copy-done | bytes 131096
  11.4 0.0 copy-start.10
  11.4 0.7 %copy-done.10 = s32[8,16]{1,0:T(8,128)S(1)} copy-done((s32[8,16]{1,0:T(8,128)S(1)}, s32[8,16]{1,0:T(8,128)}, u32[]{:S(2)}) %copy-start.10) | copy-done | bytes 536
  12.1 0.0 copy-start.11
  12.1 0.7 %copy-done.11 = s32[8,27]{1,0:T(8,128)S(1)} copy-done((s32[8,27]{1,0:T(8,128)S(1)}, s32[8,27]{1,0:T(8,128)}, u32[]{:S(2)}) %copy-start.11) | copy-done | bytes 888
  12.8 7.5 %shard_map.131 = (bf16[8,64,512]{2,1,0:T(8,128)(2,1)}, bf16[8,4,16,128]{3,2,1,0:T(8,128)(2,1)S(1)}, bf16[8,16,128]{2,1,0:T(8,128)(2,1)S(1)}, bf16[8,16,128]{2,1,0:T(8,128)(2,1)S(1)}) custom-call(s32[1]{0:T(128)} %bitcast.odd, s32[1]{0:T(128)} %bitcast.1.first, s32[8,27]{1,0:T(8,128)S(1)} %copy-done.11, s32[8,16]{1,0:T(8,128)S(1)} %copy-done.10, ...), custom_call_target="tpu_custom_call" | custom-call | tf_op jit(solution)/shard_map/pallas_call | solution.py:445
  20.2 0.0 collective-permute-start.2
  20.2 1.4 %collective-permute-start.3 = (bf16[8,16,128]{2,1,0:T(8,128)(2,1)S(1)}, bf16[8,16,128]{2,1,0:T(8,128)(2,1)S(1)}, u32[]{:S(2)}, u32[]{:S(2)}) collective-permute-start(bf16[8,16,128]{2,1,0:T(8,128)(2,1)S(1)} %get-tuple-element.16), channel_id=1, source_target_pairs={{0,16},{1,2},{2,1},{3,4},{4,3},{5,6},{6,5},{7,8},{8,7},{9,10},{10,... | collective-permute-start | bytes 98312 | tf_op jit(solution)/shard_map/ppermute | solution.py:429
  21.7 0.0 collective-permute-done.2.from_a
  21.7 2.8 %collective-permute-done.3.from_b = bf16[8,16,128]{2,1,0:T(8,128)(2,1)S(1)} collective-permute-done((bf16[8,16,128]{2,1,0:T(8,128)(2,1)S(1)}, bf16[8,16,128]{2,1,0:T(8,128)(2,1)S(1)}, u32[]{:S(2)}, u32[]{:S(2)}) %collective-permute-start.3) | collective-permute-done | bytes 32800 | tf_op jit(solution)/shard_map/ppermute | solution.py:429
  24.5 0.0 copy-start.3
  24.5 1.2 %copy-done.3 = bf16[27,128,128]{2,1,0:T(8,128)(2,1)S(1)} copy-done((bf16[27,128,128]{2,1,0:T(8,128)(2,1)S(1)}, bf16[27,128,128]{2,1,0:T(8,128)(2,1)}, u32[]{:S(2)}) %copy-start.3) | copy-done | bytes 884760
  25.6 0.0 copy-start.4
  25.6 1.0 %copy-done.4 = bf16[8,128,256]{2,1,0:T(8,128)(2,1)S(1)} copy-done((bf16[8,128,256]{2,1,0:T(8,128)(2,1)S(1)}, bf16[8,128,256]{2,1,0:T(8,128)(2,1)}, u32[]{:S(2)}) %copy-start.4) | copy-done | bytes 524312
  26.7 0.0 copy-start.8
  26.7 0.9 %copy-done.8 = bf16[144,144]{1,0:T(8,128)(2,1)S(1)} copy-done((bf16[144,144]{1,0:T(8,128)(2,1)S(1)}, bf16[144,144]{1,0:T(8,128)(2,1)}, u32[]{:S(2)}) %copy-start.8) | copy-done | bytes 41496
  27.6 0.0 copy-start.12
  27.6 0.7 %copy-done.12 = s32[8,27]{1,0:T(8,128)S(1)} copy-done((s32[8,27]{1,0:T(8,128)S(1)}, s32[8,27]{1,0:T(8,128)}, u32[]{:S(2)}) %copy-start.12) | copy-done | bytes 888
  28.3 0.0 copy-start.13
  28.3 0.7 %copy-done.13 = bf16[64,64]{1,0:T(8,128)(2,1)S(1)} copy-done((bf16[64,64]{1,0:T(8,128)(2,1)S(1)}, bf16[64,64]{1,0:T(8,128)(2,1)}, u32[]{:S(2)}) %copy-start.13) | copy-done | bytes 8216
  29.0 3.4 %shard_map.132 = (bf16[8,64,128]{2,1,0:T(8,128)(2,1)}, bf16[8,8,256]{2,1,0:T(8,128)(2,1)S(1)}) custom-call(s32[1]{0:T(128)} %bitcast.odd, s32[1]{0:T(128)} %bitcast.1.first, s32[8,27]{1,0:T(8,128)S(1)} %copy-done.12, s32[8,16]{1,0:T(8,128)S(1)} %copy-done.10, bf16[144,144]{1,0:T(8,128)(2,1)S(1)} %copy-done.8, bf16[64,64]{1,0:T(8,128)(2,1)S(1)} %copy-done.13, ...), custom_call_target="tpu_custom_call" | custom-call | tf_op jit(solution)/shard_map/pallas_call | solution.py:471
  32.3 1.4 %collective-permute-start.5 = (bf16[8,8,256]{2,1,0:T(8,128)(2,1)S(1)}, bf16[8,8,256]{2,1,0:T(8,128)(2,1)S(1)}, u32[]{:S(2)}, u32[]{:S(2)}) collective-permute-start(bf16[8,8,256]{2,1,0:T(8,128)(2,1)S(1)} %get-tuple-element.18.inputs), channel_id=1, source_target_pairs={{0,16},{1,2},{2,1},{3,4},{4,3},{5,6},{6,5},{7,8},{8,7},{9,10},{10,... | collective-permute-start | bytes 98312 | tf_op jit(solution)/shard_map/ppermute | solution.py:429
  33.8 0.0 collective-permute-start.4
  33.8 2.8 %collective-permute-done.5.from_b = bf16[8,8,256]{2,1,0:T(8,128)(2,1)S(1)} collective-permute-done((bf16[8,8,256]{2,1,0:T(8,128)(2,1)S(1)}, bf16[8,8,256]{2,1,0:T(8,128)(2,1)S(1)}, u32[]{:S(2)}, u32[]{:S(2)}) %collective-permute-start.5) | collective-permute-done | bytes 32800 | tf_op jit(solution)/shard_map/ppermute | solution.py:429
  36.6 0.0 collective-permute-done.4.from_a
  36.6 0.0 copy-done.7
  36.6 0.0 copy-start.2
  36.6 2.0 %copy-done.2 = bf16[27,256,256]{2,1,0:T(8,128)(2,1)S(1)} copy-done((bf16[27,256,256]{2,1,0:T(8,128)(2,1)S(1)}, bf16[27,256,256]{2,1,0:T(8,128)(2,1)}, u32[]{:S(2)}) %copy-start.2) | copy-done | bytes 3538968
  38.6 2.7 %shard_map.133 = bf16[8,8,256]{2,1,0:T(8,128)(2,1)} custom-call(s32[1]{0:T(128)} %bitcast.odd, s32[1]{0:T(128)} %bitcast.1.first, s32[8,27]{1,0:T(8,128)S(1)} %copy-done.12, s32[8,16]{1,0:T(8,128)S(1)} %copy-done.10, bf16[216,216]{1,0:T(8,128)(2,1)S(1)} %copy-done.7, bf16[8,8,256]{2,1,0:T(8,128)(2,1)S(1)} %get-tuple-element.18.inputs, ...), custom_call_target="tpu_custom_call" | custom-call | tf_op jit(solution)/shard_map/pallas_call | solution.py:492
Async XLA Ops:
  0.6 1.0 %copy-start = (bf16[8,512,64]{1,2,0:T(8,128)(2,1)S(1)}, bf16[8,512,64]{1,2,0:T(8,128)(2,1)}, u32[]{:S(2)}) copy-start(bf16[8,512,64]{1,2,0:T(8,128)(2,1)} %param.11) | copy-start | bytes 1572868
  1.7 0.7 %copy-start.9 = (s32[8,16]{1,0:T(8,128)S(1)}, s32[8,16]{1,0:T(8,128)}, u32[]{:S(2)}) copy-start(s32[8,16]{1,0:T(8,128)} %occupancy.7) | copy-start | bytes 1540
  2.4 34.2 %copy-start.7 = (bf16[216,216]{1,0:T(8,128)(2,1)S(1)}, bf16[216,216]{1,0:T(8,128)(2,1)}, u32[]{:S(2)}) copy-start(bf16[216,216]{1,0:T(8,128)(2,1)} %constant.27.clone.shifts) | copy-start | bytes 279940
  3.1 1.9 %collective-permute-start = (bf16[4,64,128]{2,1,0:T(8,128)(2,1)S(1)}, bf16[4,64,128]{2,1,0:T(8,128)(2,1)S(1)}, u32[]{:S(2)}, u32[]{:S(2)}) collective-permute-start(bf16[4,64,128]{2,1,0:T(8,128)(2,1)S(1)} %get-tuple-element.11), channel_id=1, source_target_pairs={{0,1},{1,0},{2,3},{3,2},{4,5},{5,4},{6,7},{7,6},{8,9},{9,8},{10,11... | collective-permute-start | bytes 196616 | tf_op jit(solution)/shard_map/ppermute | solution.py:430
  3.8 4.6 %collective-permute-start.1 = (bf16[4,64,128]{2,1,0:T(8,128)(2,1)S(1)}, bf16[4,64,128]{2,1,0:T(8,128)(2,1)S(1)}, u32[]{:S(2)}, u32[]{:S(2)}) collective-permute-start(bf16[4,64,128]{2,1,0:T(8,128)(2,1)S(1)} %get-tuple-element.12), channel_id=1, source_target_pairs={{0,16},{1,2},{2,1},{3,4},{4,3},{5,6},{6,5},{7,8},{8,7},{9,10},{10,... | collective-permute-start | bytes 196616 | tf_op jit(solution)/shard_map/ppermute | solution.py:429
  8.4 1.0 %copy-start.1 = (bf16[8,512,64]{1,2,0:T(8,128)(2,1)S(1)}, bf16[8,512,64]{1,2,0:T(8,128)(2,1)}, u32[]{:S(2)}) copy-start(bf16[8,512,64]{1,2,0:T(8,128)(2,1)} %param.11) | copy-start | bytes 1572868
  9.5 1.0 %copy-start.5 = (bf16[27,64,64]{2,1,0:T(8,128)(2,1)S(1)}, bf16[27,64,64]{2,1,0:T(8,128)(2,1)}, u32[]{:S(2)}) copy-start(bf16[27,64,64]{2,1,0:T(8,128)(2,1)} %kernel.3) | copy-start | bytes 663556
  10.5 0.9 %copy-start.6 = (bf16[8,64,128]{2,1,0:T(8,128)(2,1)S(1)}, bf16[8,64,128]{2,1,0:T(8,128)(2,1)}, u32[]{:S(2)}) copy-start(bf16[8,64,128]{2,1,0:T(8,128)(2,1)} %reduce.2) | copy-start | bytes 393220
  11.4 0.7 %copy-start.10 = (s32[8,16]{1,0:T(8,128)S(1)}, s32[8,16]{1,0:T(8,128)}, u32[]{:S(2)}) copy-start(s32[8,16]{1,0:T(8,128)} %occupancy.7) | copy-start | bytes 1540
  12.1 0.7 %copy-start.11 = (s32[8,27]{1,0:T(8,128)S(1)}, s32[8,27]{1,0:T(8,128)}, u32[]{:S(2)}) copy-start(s32[8,27]{1,0:T(8,128)} %neighbours.5) | copy-start | bytes 2596
  20.2 1.4 %collective-permute-start.2 = (bf16[8,16,128]{2,1,0:T(8,128)(2,1)S(1)}, bf16[8,16,128]{2,1,0:T(8,128)(2,1)S(1)}, u32[]{:S(2)}, u32[]{:S(2)}) collective-permute-start(bf16[8,16,128]{2,1,0:T(8,128)(2,1)S(1)} %get-tuple-element.15), channel_id=1, source_target_pairs={{0,1},{1,0},{2,3},{3,2},{4,5},{5,4},{6,7},{7,6},{8,9},{9,8},{10,11... | collective-permute-start | bytes 98312 | tf_op jit(solution)/shard_map/ppermute | solution.py:430
  20.2 4.2 %collective-permute-start.3 = (bf16[8,16,128]{2,1,0:T(8,128)(2,1)S(1)}, bf16[8,16,128]{2,1,0:T(8,128)(2,1)S(1)}, u32[]{:S(2)}, u32[]{:S(2)}) collective-permute-start(bf16[8,16,128]{2,1,0:T(8,128)(2,1)S(1)} %get-tuple-element.16), channel_id=1, source_target_pairs={{0,16},{1,2},{2,1},{3,4},{4,3},{5,6},{6,5},{7,8},{8,7},{9,10},{10,... | collective-permute-start | bytes 98312 | tf_op jit(solution)/shard_map/ppermute | solution.py:429
  24.5 1.2 %copy-start.3 = (bf16[27,128,128]{2,1,0:T(8,128)(2,1)S(1)}, bf16[27,128,128]{2,1,0:T(8,128)(2,1)}, u32[]{:S(2)}) copy-start(bf16[27,128,128]{2,1,0:T(8,128)(2,1)} %kernel.4) | copy-start | bytes 2654212
  25.6 1.0 %copy-start.4 = (bf16[8,128,256]{2,1,0:T(8,128)(2,1)S(1)}, bf16[8,128,256]{2,1,0:T(8,128)(2,1)}, u32[]{:S(2)}) copy-start(bf16[8,128,256]{2,1,0:T(8,128)(2,1)} %reduce.3) | copy-start | bytes 1572868
  26.7 0.9 %copy-start.8 = (bf16[144,144]{1,0:T(8,128)(2,1)S(1)}, bf16[144,144]{1,0:T(8,128)(2,1)}, u32[]{:S(2)}) copy-start(bf16[144,144]{1,0:T(8,128)(2,1)} %constant.25.clone.shifts) | copy-start | bytes 124420
  27.6 0.7 %copy-start.12 = (s32[8,27]{1,0:T(8,128)S(1)}, s32[8,27]{1,0:T(8,128)}, u32[]{:S(2)}) copy-start(s32[8,27]{1,0:T(8,128)} %neighbours.5) | copy-start | bytes 2596
  28.3 0.7 %copy-start.13 = (bf16[64,64]{1,0:T(8,128)(2,1)S(1)}, bf16[64,64]{1,0:T(8,128)(2,1)}, u32[]{:S(2)}) copy-start(bf16[64,64]{1,0:T(8,128)(2,1)} %constant.26.clone.children) | copy-start | bytes 24580
  32.3 4.2 %collective-permute-start.5 = (bf16[8,8,256]{2,1,0:T(8,128)(2,1)S(1)}, bf16[8,8,256]{2,1,0:T(8,128)(2,1)S(1)}, u32[]{:S(2)}, u32[]{:S(2)}) collective-permute-start(bf16[8,8,256]{2,1,0:T(8,128)(2,1)S(1)} %get-tuple-element.18.inputs), channel_id=1, source_target_pairs={{0,16},{1,2},{2,1},{3,4},{4,3},{5,6},{6,5},{7,8},{8,7},{9,10},{10,... | collective-permute-start | bytes 98312 | tf_op jit(solution)/shard_map/ppermute | solution.py:429
  33.8 2.8 %collective-permute-start.4 = (bf16[8,8,256]{2,1,0:T(8,128)(2,1)S(1)}, bf16[8,8,256]{2,1,0:T(8,128)(2,1)S(1)}, u32[]{:S(2)}, u32[]{:S(2)}) collective-permute-start(bf16[8,8,256]{2,1,0:T(8,128)(2,1)S(1)} %get-tuple-element.18.inputs), channel_id=1, source_target_pairs={{0,1},{1,0},{2,3},{3,2},{4,5},{5,4},{6,7},{7,6},{8,9},{9,8},{10,11... | collective-permute-start | bytes 98312 | tf_op jit(solution)/shard_map/ppermute | solution.py:430
  36.6 2.0 %copy-start.2 = (bf16[27,256,256]{2,1,0:T(8,128)(2,1)S(1)}, bf16[27,256,256]{2,1,0:T(8,128)(2,1)}, u32[]{:S(2)}) copy-start(bf16[27,256,256]{2,1,0:T(8,128)(2,1)} %kernel.5) | copy-start | bytes 10616836
where the time goes:
time: 41.9 us; the launch traced here: 41.3 us
  Pallas kernels  14.3 us (34%)
  local copies, waits for them, and re-layouts  12.6 us (30%)
  waiting for transfers between devices  8.99 us (21%)
  starting transfers between devices  4.82 us (12%)
  between operations  0.68 us (2%)
    unnamed x28, local copies, waits for them, and re-layouts  12.6 us
    ppermute x3, waiting for transfers between devices, exchange(): from_b = lax.ppermute(to_b, axes, outer)  8.98 us
    pallas_call x1, Pallas kernels, on_device(): pl.pallas_call(level_one_kernel, out_shape=(jax.ShapeDtypeStruct((count,...  7.47 us
    ppermute x3, starting transfers between devices, exchange(): from_b = lax.ppermute(to_b, axes, outer)  4.08 us
    pallas_call x1, Pallas kernels, on_device(): pl.pallas_call(level_two_kernel, out_shape=(jax.ShapeDtypeStruct((count,...  3.37 us
    pallas_call x1, Pallas kernels, on_device(): pl.pallas_call(level_three_kernel, out_shape=jax.ShapeDtypeStruct((count,...  2.74 us
  transfers between devices with their start and end apart: 6, of which 3 were waited for; matrix products, arithmetic and copies ran while one was open for 0% of the time, Pallas kernels for 0%

commit v1 on v0

--- a/solution.py
+++ b/solution.py
@@ -252,7 +252,7 @@
         to_b[b] = jnp.where(is_odd, planes[3], planes[0])
         return carry
 
-    lax.fori_loop(0, count, brick, 0)
+    lax.fori_loop(0, count, brick, 0, unroll=True)
 
 
 def level_two_kernel(
@@ -390,7 +390,7 @@
 
 SMEM = pl.BlockSpec(memory_space=pltpu.SMEM)
 VMEM = pl.BlockSpec(memory_space=pltpu.VMEM)
-PARAMS = pltpu.CompilerParams(vmem_limit_bytes=48 * 1024 * 1024)
+PARAMS = pltpu.CompilerParams(vmem_limit_bytes=24 * 1024 * 1024)
 
 
 def swaps(tiles, count):
@@ -438,6 +438,7 @@
         in_specs=[SMEM, SMEM, edge, pl.BlockSpec((count, 64, 128), lambda i: (0, 0, 3))],
         out_specs=(pl.BlockSpec((count // 2, 64, 128), lambda i: (0, 0, 0)),) * 2,
         compiler_params=PARAMS,
+        cost_estimate=pl.CostEstimate(flops=4 * 10**9, bytes_accessed=10**7, transcendentals=0),
     )(odd, occupancy, features, features)
     from_a, from_b = exchange(to_a, to_b)
 
@@ -462,6 +463,7 @@
             pltpu.VMEM((128, 128), F32),
         ],
         compiler_params=PARAMS,
+        cost_estimate=pl.CostEstimate(flops=4 * 10**9, bytes_accessed=10**7, transcendentals=0),
     )(
         odd, first, neighbours, occupancy, features, from_a, from_b, conv_one,
         first_reduce_kernel,
@@ -483,6 +485,7 @@
             pltpu.VMEM((9, count, 6, 16, 128), BF16),
         ],
         compiler_params=PARAMS,
+        cost_estimate=pl.CostEstimate(flops=4 * 10**9, bytes_accessed=10**7, transcendentals=0),
     )(
         odd, first, neighbours, occupancy, plane_shifts(), child_rows(), second_input,
         from_a, from_b, conv_two, second_reduce_kernel,
@@ -496,6 +499,7 @@
         out_specs=VMEM,
         scratch_shapes=[pltpu.VMEM((3, count + 1, 8, 256), F32)],
         compiler_params=PARAMS,
+        cost_estimate=pl.CostEstimate(flops=4 * 10**9, bytes_accessed=10**7, transcendentals=0),
     )(
         odd, first, neighbours, occupancy, brick_shifts(), third_input, from_a, from_b,
         conv_three,

time: 41.9 us -> 29.6 us (0.71)
  the two profiles are of different devices: /device:TPU:21 before, /device:TPU:13 now
where the time goes in v1:
time: 29.6 us; the launch traced here: 29.4 us
  Pallas kernels  13.1 us (44%)
  waiting for transfers between devices  8.99 us (30%)
  starting transfers between devices  4.82 us (16%)
  local copies, waits for them, and re-layouts  1.78 us (6%)
  between operations  0.76 us (3%)
    ppermute x3, waiting for transfers between devices, exchange(): from_b = lax.ppermute(to_b, axes, outer)  8.99 us
    pallas_call x1, Pallas kernels, on_device(): pl.pallas_call(level_one_kernel, out_shape=(jax.ShapeDtypeStruct((count,...  6.19 us
    ppermute x3, starting transfers between devices, exchange(): from_b = lax.ppermute(to_b, axes, outer)  4.07 us
    pallas_call x1, Pallas kernels, on_device(): pl.pallas_call(level_two_kernel, out_shape=(jax.ShapeDtypeStruct((count,...  3.39 us
    pallas_call x1, Pallas kernels, on_device(): pl.pallas_call(level_three_kernel, out_shape=jax.ShapeDtypeStruct((count,...  2.76 us
    unnamed x26, local copies, waits for them, and re-layouts  1.78 us
    ppermute x3, starting transfers between devices, exchange(): return (lax.ppermute(to_a, axes, inner), from_b)  0.75 us
    pallas_call x1, Pallas kernels, on_device(): pl.pallas_call(faces_kernel, grid=(1,), out_shape=(face, face), in_specs=...  0.72 us
  transfers between devices with their start and end apart: 6, of which 3 were waited for; matrix products, arithmetic and copies ran while one was open for 0% of the time, Pallas kernels for 0%

profile of v1, /device:TPU:13, one launch (start us, length us, event | category | flops | bytes accessed | tf_op | source)
XLA Modules:
  0.0 29.4 jit_solution(684349992648400906)
XLA Ops:
  0.6 0.0 copy-start.2
  0.7 1.0 %copy-done.2 = bf16[8,512,64]{1,2,0:T(8,128)(2,1)S(1)} copy-done((bf16[8,512,64]{1,2,0:T(8,128)(2,1)S(1)}, bf16[8,512,64]{1,2,0:T(8,128)(2,1)}, u32[]{:S(2)}) %copy-start.2) | copy-done | bytes 524312
  1.7 0.0 copy-start.8
  1.7 0.7 %copy-done.8 = s32[8,16]{1,0:T(8,128)S(1)} copy-done((s32[8,16]{1,0:T(8,128)S(1)}, s32[8,16]{1,0:T(8,128)}, u32[]{:S(2)}) %copy-start.8) | copy-done | bytes 536
  2.4 0.0 copy-start.3
  2.4 0.0 copy-start.5
  2.4 0.0 copy-start.6
  2.4 0.0 copy-start.7
  2.4 0.0 copy-start.9
  2.4 0.7 %shard_map.130 = (bf16[4,64,128]{2,1,0:T(8,128)(2,1)S(1)}, bf16[4,64,128]{2,1,0:T(8,128)(2,1)S(1)}) custom-call(s32[1]{0:T(128)} %bitcast.odd, s32[8,16]{1,0:T(8,128)S(1)} %copy-done.8, bf16[8,64,512]{2,1,0:T(8,128)(2,1)S(1)} %bitcast.4, bf16[8,64,512]{2,1,0:T(8,128)(2,1)S(1)} %bitcast.5), custom_call_target="tpu_custom_call" | custom-call | flops 4000000000 | bytes 10000000 | tf_op jit(solution)/shard_map/pallas_call | solution.py:434
  3.1 0.7 %collective-permute-start = (bf16[4,64,128]{2,1,0:T(8,128)(2,1)S(1)}, bf16[4,64,128]{2,1,0:T(8,128)(2,1)S(1)}, u32[]{:S(2)}, u32[]{:S(2)}) collective-permute-start(bf16[4,64,128]{2,1,0:T(8,128)(2,1)S(1)} %get-tuple-element.11), channel_id=1, source_target_pairs={{0,1},{1,0},{2,3},{3,2},{4,5},{5,4},{6,7},{7,6},{8,9},{9,8},{10,11... | collective-permute-start | bytes 196616 | tf_op jit(solution)/shard_map/ppermute | solution.py:430
  3.9 1.2 %collective-permute-start.1 = (bf16[4,64,128]{2,1,0:T(8,128)(2,1)S(1)}, bf16[4,64,128]{2,1,0:T(8,128)(2,1)S(1)}, u32[]{:S(2)}, u32[]{:S(2)}) collective-permute-start(bf16[4,64,128]{2,1,0:T(8,128)(2,1)S(1)} %get-tuple-element.12), channel_id=1, source_target_pairs={{0,16},{1,2},{2,1},{3,4},{4,3},{5,6},{6,5},{7,8},{8,7},{9,10},{10,... | collective-permute-start | bytes 196616 | tf_op jit(solution)/shard_map/ppermute | solution.py:429
  5.1 0.0 collective-permute-done.from_a
  5.1 3.4 %collective-permute-done.1.from_b = bf16[4,64,128]{2,1,0:T(8,128)(2,1)S(1)} collective-permute-done((bf16[4,64,128]{2,1,0:T(8,128)(2,1)S(1)}, bf16[4,64,128]{2,1,0:T(8,128)(2,1)S(1)}, u32[]{:S(2)}, u32[]{:S(2)}) %collective-permute-start.1) | collective-permute-done | bytes 65568 | tf_op jit(solution)/shard_map/ppermute | solution.py:429
  8.4 0.0 copy-done.3
  8.4 0.0 copy-done.5
  8.5 0.0 copy-done.6
  8.5 0.0 copy-done.7
  8.5 0.0 copy-done.9
  8.5 0.0 copy-start.1
  8.5 0.0 copy-start.4
  8.5 0.0 copy-start.11
  8.5 0.0 copy-start.12
  8.5 6.2 %shard_map.131 = (bf16[8,64,512]{2,1,0:T(8,128)(2,1)}, bf16[8,4,16,128]{3,2,1,0:T(8,128)(2,1)S(1)}, bf16[8,16,128]{2,1,0:T(8,128)(2,1)S(1)}, bf16[8,16,128]{2,1,0:T(8,128)(2,1)S(1)}) custom-call(s32[1]{0:T(128)} %bitcast.odd, s32[1]{0:T(128)} %bitcast.1.first, s32[8,27]{1,0:T(8,128)S(1)} %copy-done.7, s32[8,16]{1,0:T(8,128)S(1)} %copy-done.9, ...), custom_call_target="tpu_custom_call" | custom-call | flops 4000000000 | bytes 10000000 | tf_op jit(solution)/shard_map/pallas_call | solution.py:446
  14.7 0.0 collective-permute-start.2
  14.7 1.4 %collective-permute-start.3 = (bf16[8,16,128]{2,1,0:T(8,128)(2,1)S(1)}, bf16[8,16,128]{2,1,0:T(8,128)(2,1)S(1)}, u32[]{:S(2)}, u32[]{:S(2)}) collective-permute-start(bf16[8,16,128]{2,1,0:T(8,128)(2,1)S(1)} %get-tuple-element.16), channel_id=1, source_target_pairs={{0,16},{1,2},{2,1},{3,4},{4,3},{5,6},{6,5},{7,8},{8,7},{9,10},{10,... | collective-permute-start | bytes 98312 | tf_op jit(solution)/shard_map/ppermute | solution.py:429
  16.2 0.0 collective-permute-done.2.from_a
  16.2 2.8 %collective-permute-done.3.from_b = bf16[8,16,128]{2,1,0:T(8,128)(2,1)S(1)} collective-permute-done((bf16[8,16,128]{2,1,0:T(8,128)(2,1)S(1)}, bf16[8,16,128]{2,1,0:T(8,128)(2,1)S(1)}, u32[]{:S(2)}, u32[]{:S(2)}) %collective-permute-start.3) | collective-permute-done | bytes 32800 | tf_op jit(solution)/shard_map/ppermute | solution.py:429
  19.0 0.0 copy-done.1
  19.0 0.0 copy-done.4
  19.0 0.0 copy-done.11
  19.0 0.0 copy-done.12
  19.0 0.0 copy-start
  19.0 0.0 copy-start.10
  19.0 3.4 %shard_map.132 = (bf16[8,64,128]{2,1,0:T(8,128)(2,1)}, bf16[8,8,256]{2,1,0:T(8,128)(2,1)S(1)}) custom-call(s32[1]{0:T(128)} %bitcast.odd, s32[1]{0:T(128)} %bitcast.1.first, s32[8,27]{1,0:T(8,128)S(1)} %copy-done.7, s32[8,16]{1,0:T(8,128)S(1)} %copy-done.9, bf16[144,144]{1,0:T(8,128)(2,1)S(1)} %copy-done.11, bf16[64,64]{1,0:T(8,128)(2,1)S(1)} %copy-done.12, ...), custom_call_target="tpu_custom_call" | custom-call | flops 4000000000 | bytes 10000000 | tf_op jit(solution)/shard_map/pallas_call | solution.py:473
  22.4 1.4 %collective-permute-start.5 = (bf16[8,8,256]{2,1,0:T(8,128)(2,1)S(1)}, bf16[8,8,256]{2,1,0:T(8,128)(2,1)S(1)}, u32[]{:S(2)}, u32[]{:S(2)}) collective-permute-start(bf16[8,8,256]{2,1,0:T(8,128)(2,1)S(1)} %get-tuple-element.18.inputs), channel_id=1, source_target_pairs={{0,16},{1,2},{2,1},{3,4},{4,3},{5,6},{6,5},{7,8},{8,7},{9,10},{10,... | collective-permute-start | bytes 98312 | tf_op jit(solution)/shard_map/ppermute | solution.py:429
  23.8 0.0 collective-permute-start.4
  23.8 2.8 %collective-permute-done.5.from_b = bf16[8,8,256]{2,1,0:T(8,128)(2,1)S(1)} collective-permute-done((bf16[8,8,256]{2,1,0:T(8,128)(2,1)S(1)}, bf16[8,8,256]{2,1,0:T(8,128)(2,1)S(1)}, u32[]{:S(2)}, u32[]{:S(2)}) %collective-permute-start.5) | collective-permute-done | bytes 32800 | tf_op jit(solution)/shard_map/ppermute | solution.py:429
  26.6 0.0 collective-permute-done.4.from_a
  26.6 0.0 copy-done
  26.6 0.0 copy-done.10
  26.6 2.8 %shard_map.133 = bf16[8,8,256]{2,1,0:T(8,128)(2,1)} custom-call(s32[1]{0:T(128)} %bitcast.odd, s32[1]{0:T(128)} %bitcast.1.first, s32[8,27]{1,0:T(8,128)S(1)} %copy-done.7, s32[8,16]{1,0:T(8,128)S(1)} %copy-done.9, bf16[216,216]{1,0:T(8,128)(2,1)S(1)} %copy-done.10, bf16[8,8,256]{2,1,0:T(8,128)(2,1)S(1)} %get-tuple-element.18.inputs, ...), custom_call_target="tpu_custom_call" | custom-call | flops 4000000000 | bytes 10000000 | tf_op jit(solution)/shard_map/pallas_call | solution.py:495
Async XLA Ops:
  0.6 1.0 %copy-start.2 = (bf16[8,512,64]{1,2,0:T(8,128)(2,1)S(1)}, bf16[8,512,64]{1,2,0:T(8,128)(2,1)}, u32[]{:S(2)}) copy-start(bf16[8,512,64]{1,2,0:T(8,128)(2,1)} %param.11) | copy-start | bytes 1572868
  1.7 0.7 %copy-start.8 = (s32[8,16]{1,0:T(8,128)S(1)}, s32[8,16]{1,0:T(8,128)}, u32[]{:S(2)}) copy-start(s32[8,16]{1,0:T(8,128)} %occupancy.7) | copy-start | bytes 1540
  2.4 6.1 %copy-start.3 = (bf16[8,512,64]{1,2,0:T(8,128)(2,1)S(1)}, bf16[8,512,64]{1,2,0:T(8,128)(2,1)}, u32[]{:S(2)}) copy-start(bf16[8,512,64]{1,2,0:T(8,128)(2,1)} %param.11) | copy-start | bytes 1572868
  2.4 6.1 %copy-start.5 = (bf16[27,64,64]{2,1,0:T(8,128)(2,1)S(1)}, bf16[27,64,64]{2,1,0:T(8,128)(2,1)}, u32[]{:S(2)}) copy-start(bf16[27,64,64]{2,1,0:T(8,128)(2,1)} %kernel.3) | copy-start | bytes 663556
  2.4 6.1 %copy-start.6 = (bf16[8,64,128]{2,1,0:T(8,128)(2,1)S(1)}, bf16[8,64,128]{2,1,0:T(8,128)(2,1)}, u32[]{:S(2)}) copy-start(bf16[8,64,128]{2,1,0:T(8,128)(2,1)} %reduce.2) | copy-start | bytes 393220
  2.4 6.1 %copy-start.7 = (s32[8,27]{1,0:T(8,128)S(1)}, s32[8,27]{1,0:T(8,128)}, u32[]{:S(2)}) copy-start(s32[8,27]{1,0:T(8,128)} %neighbours.5) | copy-start | bytes 2596
  2.4 6.1 %copy-start.9 = (s32[8,16]{1,0:T(8,128)S(1)}, s32[8,16]{1,0:T(8,128)}, u32[]{:S(2)}) copy-start(s32[8,16]{1,0:T(8,128)} %occupancy.7) | copy-start | bytes 1540
  3.1 1.9 %collective-permute-start = (bf16[4,64,128]{2,1,0:T(8,128)(2,1)S(1)}, bf16[4,64,128]{2,1,0:T(8,128)(2,1)S(1)}, u32[]{:S(2)}, u32[]{:S(2)}) collective-permute-start(bf16[4,64,128]{2,1,0:T(8,128)(2,1)S(1)} %get-tuple-element.11), channel_id=1, source_target_pairs={{0,1},{1,0},{2,3},{3,2},{4,5},{5,4},{6,7},{7,6},{8,9},{9,8},{10,11... | collective-permute-start | bytes 196616 | tf_op jit(solution)/shard_map/ppermute | solution.py:430
  3.9 4.6 %collective-permute-start.1 = (bf16[4,64,128]{2,1,0:T(8,128)(2,1)S(1)}, bf16[4,64,128]{2,1,0:T(8,128)(2,1)S(1)}, u32[]{:S(2)}, u32[]{:S(2)}) collective-permute-start(bf16[4,64,128]{2,1,0:T(8,128)(2,1)S(1)} %get-tuple-element.12), channel_id=1, source_target_pairs={{0,16},{1,2},{2,1},{3,4},{4,3},{5,6},{6,5},{7,8},{8,7},{9,10},{10,... | collective-permute-start | bytes 196616 | tf_op jit(solution)/shard_map/ppermute | solution.py:429
  8.5 10.5 %copy-start.1 = (bf16[27,128,128]{2,1,0:T(8,128)(2,1)S(1)}, bf16[27,128,128]{2,1,0:T(8,128)(2,1)}, u32[]{:S(2)}) copy-start(bf16[27,128,128]{2,1,0:T(8,128)(2,1)} %kernel.4) | copy-start | bytes 2654212
  8.5 10.5 %copy-start.4 = (bf16[8,128,256]{2,1,0:T(8,128)(2,1)S(1)}, bf16[8,128,256]{2,1,0:T(8,128)(2,1)}, u32[]{:S(2)}) copy-start(bf16[8,128,256]{2,1,0:T(8,128)(2,1)} %reduce.3) | copy-start | bytes 1572868
  8.5 10.5 %copy-start.11 = (bf16[144,144]{1,0:T(8,128)(2,1)S(1)}, bf16[144,144]{1,0:T(8,128)(2,1)}, u32[]{:S(2)}) copy-start(bf16[144,144]{1,0:T(8,128)(2,1)} %constant.25.clone.shifts) | copy-start | bytes 124420
  8.5 10.5 %copy-start.12 = (bf16[64,64]{1,0:T(8,128)(2,1)S(1)}, bf16[64,64]{1,0:T(8,128)(2,1)}, u32[]{:S(2)}) copy-start(bf16[64,64]{1,0:T(8,128)(2,1)} %constant.26.clone.children) | copy-start | bytes 24580
  14.7 1.4 %collective-permute-start.2 = (bf16[8,16,128]{2,1,0:T(8,128)(2,1)S(1)}, bf16[8,16,128]{2,1,0:T(8,128)(2,1)S(1)}, u32[]{:S(2)}, u32[]{:S(2)}) collective-permute-start(bf16[8,16,128]{2,1,0:T(8,128)(2,1)S(1)} %get-tuple-element.15), channel_id=1, source_target_pairs={{0,1},{1,0},{2,3},{3,2},{4,5},{5,4},{6,7},{7,6},{8,9},{9,8},{10,11... | collective-permute-start | bytes 98312 | tf_op jit(solution)/shard_map/ppermute | solution.py:430
  14.7 4.2 %collective-permute-start.3 = (bf16[8,16,128]{2,1,0:T(8,128)(2,1)S(1)}, bf16[8,16,128]{2,1,0:T(8,128)(2,1)S(1)}, u32[]{:S(2)}, u32[]{:S(2)}) collective-permute-start(bf16[8,16,128]{2,1,0:T(8,128)(2,1)S(1)} %get-tuple-element.16), channel_id=1, source_target_pairs={{0,16},{1,2},{2,1},{3,4},{4,3},{5,6},{6,5},{7,8},{8,7},{9,10},{10,... | collective-permute-start | bytes 98312 | tf_op jit(solution)/shard_map/ppermute | solution.py:429
  19.0 7.7 %copy-start = (bf16[27,256,256]{2,1,0:T(8,128)(2,1)S(1)}, bf16[27,256,256]{2,1,0:T(8,128)(2,1)}, u32[]{:S(2)}) copy-start(bf16[27,256,256]{2,1,0:T(8,128)(2,1)} %kernel.5) | copy-start | bytes 10616836
  19.0 7.6 %copy-start.10 = (bf16[216,216]{1,0:T(8,128)(2,1)S(1)}, bf16[216,216]{1,0:T(8,128)(2,1)}, u32[]{:S(2)}) copy-start(bf16[216,216]{1,0:T(8,128)(2,1)} %constant.27.clone.shifts) | copy-start | bytes 279940
  22.4 4.2 %collective-permute-start.5 = (bf16[8,8,256]{2,1,0:T(8,128)(2,1)S(1)}, bf16[8,8,256]{2,1,0:T(8,128)(2,1)S(1)}, u32[]{:S(2)}, u32[]{:S(2)}) collective-permute-start(bf16[8,8,256]{2,1,0:T(8,128)(2,1)S(1)} %get-tuple-element.18.inputs), channel_id=1, source_target_pairs={{0,16},{1,2},{2,1},{3,4},{4,3},{5,6},{6,5},{7,8},{8,7},{9,10},{10,... | collective-permute-start | bytes 98312 | tf_op jit(solution)/shard_map/ppermute | solution.py:429
  23.8 2.8 %collective-permute-start.4 = (bf16[8,8,256]{2,1,0:T(8,128)(2,1)S(1)}, bf16[8,8,256]{2,1,0:T(8,128)(2,1)S(1)}, u32[]{:S(2)}, u32[]{:S(2)}) collective-permute-start(bf16[8,8,256]{2,1,0:T(8,128)(2,1)S(1)} %get-tuple-element.18.inputs), channel_id=1, source_target_pairs={{0,1},{1,0},{2,3},{3,2},{4,5},{5,4},{6,7},{7,6},{8,9},{9,8},{10,11... | collective-permute-start | bytes 98312 | tf_op jit(solution)/shard_map/ppermute | solution.py:430
